TPU v7x, 512 devices: a whole 4x4x16 slice. The times are simulated.
512 devices in a mesh: date: 8 (over z_lo), tile: 64 (over z_hi, y, x, core).
Axes of the slice: x: 4, y: 4, z: 16 (z_hi: 2, z_lo: 8; z = z_hi * 8 + z_lo), core: 2. Of those that a mesh axis runs over, the one named last changes fastest.
Arguments:
- reflectance: bfloat16 [72, 10, 512, 1024], P('date', None, 'tile'), may hold values from 0 to 0.59765625
- clear_mask: int32 [72, 512, 1024], P('date', 'tile'), may hold values from 0 to 1, as said below
- time_kernel: float32 [5], replicated, may hold values from 0.25 to 1
- space_kernel: float32 [5], replicated, may hold values from 0.25 to 1
Outputs:
- filled_bands: bfloat16 [72, 10, 512, 1024], P('date', None, 'tile')
- coefficients: float32 [12, 24, 512, 1024], P(None, None, 'tile', 'date')
Inputs may be any that keep to these rules, and one draw needn't show every extreme that they name: `clear_mask`: cloud cover differs strongly between strips of 8 rows and between dates.
All inputs are finite; a program needn't handle non-finite values.
Results may differ from a plain program's by a relative error of at most 0.0065.
Values may be sent and summed in bfloat16 or wider, within the bound.
A program may use at most 128 MiB of HBM per device.

v0:
```python
import math

import jax
import jax.numpy as jnp
from jax import lax
from jax.sharding import PartitionSpec as P

TERMS = 24


def padded(block, sides, width):
    for axis, dim in sides:
        count = lax.axis_size(axis)
        forward = [(i, i + 1) for i in range(count - 1)]
        backward = [(target, source) for source, target in forward]
        low = lax.ppermute(
            lax.slice_in_dim(block, block.shape[dim] - width, None, axis=dim), axis, forward
        )
        high = lax.ppermute(lax.slice_in_dim(block, 0, width, axis=dim), axis, backward)
        block = jnp.concatenate([low, block, high], axis=dim)
    return block


def fit_matrix(dates, terms):
    steps = jnp.arange(dates, dtype=jnp.float32)
    columns = [jnp.ones((dates,), jnp.float32), steps / dates - 0.5]
    for order in range(1, (terms - 2) // 2 + 1):
        angle = 2.0 * math.pi * order * steps / dates
        columns.append(jnp.cos(angle))
        columns.append(jnp.sin(angle))
    basis = jnp.stack(columns, axis=1)
    gram = jnp.dot(basis.T, basis, precision=lax.Precision.HIGHEST)
    factor = jnp.linalg.cholesky(gram)
    return jax.scipy.linalg.cho_solve((factor, True), basis.T)


def column_band(space_kernel, cols):
    source = lax.broadcasted_iota(jnp.int32, (cols, cols), 0)
    target = lax.broadcasted_iota(jnp.int32, (cols, cols), 1)
    offset = source - target
    band = jnp.zeros((cols, cols), jnp.float32)
    for k in range(5):
        band = band + jnp.where(offset == k - 2, space_kernel[k], 0.0)
    return band


def smooth_block(widened, time_kernel, space_kernel, dates, rows, cols):
    timed = sum((time_kernel[i] * widened[i : i + dates].astype(jnp.float32) for i in range(5)))
    rowed = sum((space_kernel[j] * timed[:, j : j + rows] for j in range(5)))
    band = column_band(space_kernel, cols)
    return jnp.dot(rowed, band, precision=lax.Precision.HIGHEST, preferred_element_type=jnp.float32)


def add_indices(bands):
    red = bands[:, 2].astype(jnp.float32)
    near = bands[:, 6].astype(jnp.float32)
    swir = bands[:, 8].astype(jnp.float32)
    savi = (1.5 * (near - red) / (near + red + 0.5)).astype(jnp.bfloat16)
    moisture = ((near - swir) / (near + swir + 0.5)).astype(jnp.bfloat16)
    return jnp.concatenate([bands, savi[:, None], moisture[:, None]], axis=1)


def per_device(reflectance, clear_mask, time_kernel, space_kernel):
    dates, bands, rows, cols = reflectance.shape
    clear_low = clear_mask.astype(jnp.bfloat16)
    masked = jnp.transpose(reflectance * clear_low[:, None], (0, 2, 1, 3))
    stacked = jnp.concatenate([masked, clear_low[:, :, None]], axis=2)
    widened = padded(stacked, (("date", 0), ("tile", 1)), 2)
    smoothed = smooth_block(widened, time_kernel, space_kernel, dates, rows, cols)
    weighted_sum = jnp.transpose(smoothed[:, :, :bands], (0, 2, 1, 3))
    weight_total = smoothed[:, :, bands][:, None]
    clear = clear_mask.astype(jnp.float32)[:, None]
    values = reflectance.astype(jnp.float32)
    filled = (clear * values + (1.0 - clear) * weighted_sum / (weight_total + 1.0)).astype(
        jnp.bfloat16
    )
    fitting = fit_matrix(dates * lax.axis_size("date"), TERMS)
    fit_high = fitting.astype(jnp.bfloat16)
    fit_rest = (fitting - fit_high.astype(jnp.float32)).astype(jnp.bfloat16)
    series = add_indices(filled)
    project_series = lax.all_to_all(series, "date", split_axis=3, concat_axis=0, tiled=True)
    steps, channels, strip_rows, width = project_series.shape
    flat = project_series.reshape(steps, channels * strip_rows * width)
    result = jnp.dot(fit_high, flat, preferred_element_type=jnp.float32)
    result = result + jnp.dot(fit_rest, flat, preferred_element_type=jnp.float32)
    result = result.reshape(fit_high.shape[0], channels, strip_rows, width)
    coefficients = jnp.transpose(result, (1, 0, 2, 3))
    return (filled, coefficients)


def solution(mesh):
    placed = (P("date", None, "tile", None), P("date", "tile", None), P(), P())
    return jax.shard_map(
        per_device,
        mesh=mesh,
        in_specs=placed,
        out_specs=(P("date", None, "tile", None), P(None, None, "tile", "date")),
        check_vma=False,
    )
```

profile of v0, /device:TPU:8, one launch (start us, length us, event | category | flops | bytes accessed | tf_op | source)
XLA Modules:
  0.0 294.7 jit_solution(9313248187134623153)
XLA Ops:
  0.6 1.1 fusion.86
  1.7 1.5 multiply_bitcast_fusion
  3.3 4.0 %collective-permute-start = (bf16[2,8,11,1024]{3,1,2,0:T(8,128)(2,1)S(1)}, bf16[2,8,11,1024]{3,1,2,0:T(8,128)(2,1)S(1)}, u32[]{:S(2)}, u32[]{:S(2)}) collective-permute-start(bf16[2,8,11,1024]{3,1,2,0:T(8,128)(2,1)S(1)} %get-tuple-element.10), channel_id=1, source_target_pairs={{0,64},{64,128},{128,192},{192,256},{256,320},{320,384},{384,448},... | collective-permute-start | bytes 1081352 | tf_op jit(solution)/shard_map/ppermute | solution.py:16
  7.3 1.3 collective-permute-start.1
  8.6 6.3 %collective-permute-done = bf16[2,8,11,1024]{3,1,2,0:T(8,128)(2,1)S(1)} collective-permute-done((bf16[2,8,11,1024]{3,1,2,0:T(8,128)(2,1)S(1)}, bf16[2,8,11,1024]{3,1,2,0:T(8,128)(2,1)S(1)}, u32[]{:S(2)}, u32[]{:S(2)}) %collective-permute-start) | collective-permute-done | bytes 360480 | tf_op jit(solution)/shard_map/ppermute | solution.py:16
  15.0 4.3 %collective-permute-done.1 = bf16[2,8,11,1024]{3,1,2,0:T(8,128)(2,1)S(1)} collective-permute-done((bf16[2,8,11,1024]{3,1,2,0:T(8,128)(2,1)S(1)}, bf16[2,8,11,1024]{3,1,2,0:T(8,128)(2,1)S(1)}, u32[]{:S(2)}, u32[]{:S(2)}) %collective-permute-start.1) | collective-permute-done | bytes 360480 | tf_op jit(solution)/shard_map/ppermute | solution.py:19
  20.3 1.9 collective-permute-start.2
  22.2 5.8 %collective-permute-start.3 = (bf16[13,2,11,1024]{3,1,2,0:T(2,128)(2,1)S(1)}, bf16[13,2,11,1024]{3,1,2,0:T(2,128)(2,1)S(1)}, u32[]{:S(2)}, u32[]{:S(2)}) collective-permute-start(bf16[13,2,11,1024]{3,1,2,0:T(2,128)(2,1)S(1)} %get-tuple-element.9), channel_id=1, source_target_pairs={{1,0},{2,1},{3,2},{4,3},{5,4},{6,5},{7,6},{8,7},{9,8},{10,9},{11,1... | collective-permute-start | bytes 1757192 | tf_op jit(solution)/shard_map/ppermute | solution.py:19
  29.4 4.2 %collective-permute-done.2 = bf16[13,2,11,1024]{3,1,2,0:T(2,128)(2,1)S(1)} collective-permute-done((bf16[13,2,11,1024]{3,1,2,0:T(2,128)(2,1)S(1)}, bf16[13,2,11,1024]{3,1,2,0:T(2,128)(2,1)S(1)}, u32[]{:S(2)}, u32[]{:S(2)}) %collective-permute-start.2) | collective-permute-done | bytes 585760 | tf_op jit(solution)/shard_map/ppermute | solution.py:16
  33.6 1.8 collective-permute-done.3
  35.3 3.8 %pad_maximum_fusion = bf16[13,12,11,1024]{3,1,2,0:T(8,128)(2,1)S(1)} fusion(bf16[13,2,11,1024]{3,1,2,0:T(2,128)(2,1)S(1)} %collective-permute-done.3, bf16[2,8,11,1024]{3,1,2,0:T(8,128)(2,1)S(1)} %collective-permute-done.1, bf16[9,8,1,1024]{3,1,2,0:T(8,128)(2,1)S(1)} %bitcast.68, bf16[9,8,10,1024]{3,1,2,0:T(8,128)(2,1)S(1)} %multiply_bitcast_fusion, ...), kind=kLoop, calls=%fused_computation.4 | loop fusion | flops 21086208 | bytes 7028736 | tf_op jit(solution)/shard_map/concatenate | solution.py:20
  39.1 7.0 %multiply_add_fusion = f32[9,12,11,1024]{3,1,2,0:T(8,128)S(1)} fusion(bf16[13,12,11,1024]{3,1,2,0:T(8,128)(2,1)S(1)} %pad_maximum_fusion, f32[]{:T(128)} %bitcast.8, f32[]{:T(128)} %bitcast.7, f32[]{:T(128)} %bitcast.6, f32[]{:T(128)} %bitcast.5, f32[]{:T(128)} %bitcast.1), kind=kLoop, calls=%fused_computation.1 | loop fusion | flops 17031168 | bytes 17031188 | tf_op jit(solution)/shard_map/add | solution.py:48
  46.2 5.3 %fusion.22 = f32[9,8,11,1024]{3,1,2,0:T(8,128)S(1)} fusion(f32[9,12,11,1024]{3,1,2,0:T(8,128)S(1)} %multiply_add_fusion, f32[]{:T(128)} %bitcast.12, f32[]{:T(128)} %bitcast.11, f32[]{:T(128)} %bitcast.10, f32[]{:T(128)} %bitcast.9, f32[]{:T(128)} %bitcast), kind=kLoop, calls=%fused_computation.22 | loop fusion | flops 7299072 | bytes 19464212 | tf_op jit(solution)/shard_map/add | solution.py:49
  51.4 20.5 %fusion = f32[9,8,11,1024]{3,2,1,0:T(8,128)S(1)} fusion(f32[9,8,11,1024]{3,1,2,0:T(8,128)S(1)} %fusion.22, f32[]{:T(128)} %bitcast.12, f32[]{:T(128)} %bitcast.11, f32[]{:T(128)} %bitcast.10, f32[]{:T(128)} %bitcast.9, f32[]{:T(128)} %bitcast), kind=kOutput, calls=%fused_computation.2 | convolution fusion | flops 9981394944 | bytes 6488084 | tf_op jit(solution)/shard_map/dot_general | solution.py:51
  72.4 3.0 %fusion.29 = bf16[9,10,8,1024]{3,2,1,0:T(8,128)(2,1)S(1)} fusion(f32[9,8,10,1024]{3,2,1,0:T(8,128)S(1)} %bitcast.64, bf16[9,10,8,1024]{3,2,1,0:T(8,128)(2,1)S(1)} %copy-done.1, f32[9,8,1024]{2,1,0:T(8,128)S(1)} %bitcast.69, f32[9,8,1024]{2,1,0:T(8,128)S(1)} %broadcast_subtract_fusion, f32[9,8,1024]{2,1,0:T(8,128)S(1)} %get-tuple-element.14), kind=kLoop, calls=%fused_computation.34 | loop fusion | flops 4423680 | bytes 6782976 | tf_op jit(solution)/shard_map/convert_element_type | solution.py:74
  75.8 16.2 %copy.33 = bf16[9,12,8,1024]{1,2,0,3:T(8,128)(2,1)} copy(bf16[9,12,8,1024]{3,2,1,0:T(8,128)(2,1)S(1)} %pad_maximum_fusion.1) | data formatting | bytes 3538944 | tf_op jit(solution)/shard_map/concatenate | solution.py:60
  92.0 41.4 %reshape.204 = bf16[8,2,55296]{2,1,0:T(2,128)(2,1)} reshape(bf16[1024,9,8,12]{3,2,1,0:T(8,128)(2,1)} %bitcast.62) | data formatting | bytes 3538944
  133.5 11.0 %all-to-all-start = ((bf16[8,2,55296]{2,1,0:T(2,128)(2,1)}), bf16[8,2,55296]{2,1,0:T(2,128)(2,1)S(1)}, u32[]{:S(2)}, u32[]{:S(2)}) async-start(bf16[8,2,55296]{2,1,0:T(2,128)(2,1)} %reshape.204), calls=%async_computation | async-start | bytes 3538944 | tf_op jit(solution)/shard_map/all_to_all | solution.py:81
  145.3 2.2 cholesky.16
  148.9 1.8 custom-call.10
  151.1 75.3 %all-to-all-done = bf16[8,2,55296]{2,1,0:T(2,128)(2,1)S(1)} async-done(((bf16[8,2,55296]{2,1,0:T(2,128)(2,1)}), bf16[8,2,55296]{2,1,0:T(2,128)(2,1)S(1)}, u32[]{:S(2)}, u32[]{:S(2)}) %all-to-all-start) | async-done | bytes 1769504 | tf_op jit(solution)/shard_map/all_to_all | solution.py:81
  226.4 45.6 %reshape.205 = bf16[1024,9,8,12]{3,2,1,0:T(8,128)(2,1)} reshape(bf16[8,2,55296]{2,1,0:T(2,128)(2,1)S(1)} %all-to-all-done) | data formatting | bytes 3538944
  272.0 19.6 %copy.35 = bf16[8,9,12,8,128]{4,3,2,1,0:T(8,128)(2,1)S(1)} copy(bf16[8,9,12,8,128]{2,3,1,4,0:T(8,128)(2,1)} %bitcast.63) | data formatting | bytes 3538944 | tf_op jit(solution)/shard_map/all_to_all | solution.py:81
  293.6 1.1 copy.56
  (45 shorter events, 7.6 us)
Async XLA Ops:
  3.2 24.8 %copy-start.3 = (f32[5]{0:T(128)S(1)}, f32[5]{0:T(128)}, u32[]{:S(2)}) copy-start(f32[5]{0:T(128)} %param.6) | copy-start | bytes 64
  3.2 25.4 %copy-start.4 = (f32[5]{0:T(128)S(1)}, f32[5]{0:T(128)}, u32[]{:S(2)}) copy-start(f32[5]{0:T(128)} %param.7) | copy-start | bytes 64
  3.3 26.1 %copy-start.2 = (s32[9,8,1024]{2,1,0:T(8,128)S(1)}, s32[9,8,1024]{2,1,0:T(8,128)}, u32[]{:S(2)}) copy-start(s32[9,8,1024]{2,1,0:T(8,128)} %param.5) | copy-start | bytes 884740
  3.3 11.6 %collective-permute-start = (bf16[2,8,11,1024]{3,1,2,0:T(8,128)(2,1)S(1)}, bf16[2,8,11,1024]{3,1,2,0:T(8,128)(2,1)S(1)}, u32[]{:S(2)}, u32[]{:S(2)}) collective-permute-start(bf16[2,8,11,1024]{3,1,2,0:T(8,128)(2,1)S(1)} %get-tuple-element.10), channel_id=1, source_target_pairs={{0,64},{64,128},{128,192},{192,256},{256,320},{320,384},{384,448},... | collective-permute-start | bytes 1081352 | tf_op jit(solution)/shard_map/ppermute | solution.py:16
  7.3 11.9 %collective-permute-start.1 = (bf16[2,8,11,1024]{3,1,2,0:T(8,128)(2,1)S(1)}, bf16[2,8,11,1024]{3,1,2,0:T(8,128)(2,1)S(1)}, u32[]{:S(2)}, u32[]{:S(2)}) collective-permute-start(bf16[2,8,11,1024]{3,1,2,0:T(8,128)(2,1)S(1)} %get-tuple-element.11), channel_id=1, source_target_pairs={{64,0},{128,64},{192,128},{256,192},{320,256},{384,320},{448,384},... | collective-permute-start | bytes 1081352 | tf_op jit(solution)/shard_map/ppermute | solution.py:19
  20.3 13.3 %collective-permute-start.2 = (bf16[13,2,11,1024]{3,1,2,0:T(2,128)(2,1)S(1)}, bf16[13,2,11,1024]{3,1,2,0:T(2,128)(2,1)S(1)}, u32[]{:S(2)}, u32[]{:S(2)}) collective-permute-start(bf16[13,2,11,1024]{3,1,2,0:T(2,128)(2,1)S(1)} %get-tuple-element.8), channel_id=1, source_target_pairs={{0,1},{1,2},{2,3},{3,4},{4,5},{5,6},{6,7},{7,8},{8,9},{9,10},{10,1... | collective-permute-start | bytes 1757192 | tf_op jit(solution)/shard_map/ppermute | solution.py:16
  22.2 13.1 %collective-permute-start.3 = (bf16[13,2,11,1024]{3,1,2,0:T(2,128)(2,1)S(1)}, bf16[13,2,11,1024]{3,1,2,0:T(2,128)(2,1)S(1)}, u32[]{:S(2)}, u32[]{:S(2)}) collective-permute-start(bf16[13,2,11,1024]{3,1,2,0:T(2,128)(2,1)S(1)} %get-tuple-element.9), channel_id=1, source_target_pairs={{1,0},{2,1},{3,2},{4,3},{5,4},{6,5},{7,6},{8,7},{9,8},{10,9},{11,1... | collective-permute-start | bytes 1757192 | tf_op jit(solution)/shard_map/ppermute | solution.py:19
  51.4 20.9 %copy-start.1 = (bf16[9,10,8,1024]{3,2,1,0:T(8,128)(2,1)S(1)}, bf16[9,10,8,1024]{3,2,1,0:T(8,128)(2,1)}, u32[]{:S(2)}) copy-start(bf16[9,10,8,1024]{3,2,1,0:T(8,128)(2,1)} %param.4) | copy-start | bytes 4423684
  75.4 16.6 %copy-start = (bf16[9,10,8,1024]{3,2,1,0:T(8,128)(2,1)}, bf16[9,10,8,1024]{3,2,1,0:T(8,128)(2,1)S(1)}, u32[]{:S(2)}) copy-start(bf16[9,10,8,1024]{3,2,1,0:T(8,128)(2,1)S(1)} %fusion.29) | copy-start | bytes 4423684
  133.5 92.9 %all-to-all-start = ((bf16[8,2,55296]{2,1,0:T(2,128)(2,1)}), bf16[8,2,55296]{2,1,0:T(2,128)(2,1)S(1)}, u32[]{:S(2)}, u32[]{:S(2)}) async-start(bf16[8,2,55296]{2,1,0:T(2,128)(2,1)} %reshape.204), calls=%async_computation | async-start | bytes 3538944 | tf_op jit(solution)/shard_map/all_to_all | solution.py:81
where the time goes:
time: 295 us
  local copies, waits for them, and re-layouts  127 us (43%)
  waiting for transfers between devices  91.9 us (31%)
  other arithmetic  29.4 us (10%)
  starting transfers between devices  23.9 us (8%)
  matrix products  21.9 us (7%)
    unnamed x14, local copies, waits for them, and re-layouts  87.4 us
    all_to_all x1, waiting for transfers between devices, per_device(): lax.all_to_all(series, 'date', split_axis=3, concat_axis=0, tiled=True)  75.3 us
    dot_general x1, matrix products, smooth_block(): jnp.dot(rowed, band, precision=lax.Precision.HIGHEST, preferred_element_t...  20.5 us
    all_to_all x1, local copies, waits for them, and re-layouts, per_device(): lax.all_to_all(series, 'date', split_axis=3, concat_axis=0, tiled=True)  19.6 us
    concatenate x1, local copies, waits for them, and re-layouts, add_indices(): return jnp.concatenate([bands, savi[:, None], moisture[:, None]], axis=1)  16.2 us
    all_to_all x1, starting transfers between devices, per_device(): lax.all_to_all(series, 'date', split_axis=3, concat_axis=0, tiled=True)  11 us
    ppermute x2, waiting for transfers between devices, padded(): lax.ppermute(lax.slice_in_dim(block, block.shape[dim] - width, None, axis...  10.5 us
    add x1, other arithmetic, smooth_block(): sum((time_kernel[i] * widened[i:i + dates].astype(jnp.float32) for i in r...  7.05 us
  transfers between devices with their start and end apart: 5, of which 5 were waited for; matrix products, arithmetic and copies ran while one was open for 3% of the time, Pallas kernels for 0%

commit v1 on v0

v1 whole, which is shorter than its diff:
```python
import functools
import math

import jax
import jax.numpy as jnp
import numpy as np
from jax import lax
from jax.experimental import pallas as pl
from jax.experimental.pallas import tpu as pltpu
from jax.sharding import PartitionSpec as P

TERMS = 24
PACK = 32
AHEAD = 4
MESH = pl.DeviceIdType.MESH
F32 = jnp.float32
BF16 = jnp.bfloat16


def fit_matrix(dates, terms):
    steps = np.arange(dates, dtype=np.float64)
    columns = [np.ones((dates,)), steps / dates - 0.5]
    for order in range(1, (terms - 2) // 2 + 1):
        angle = 2.0 * math.pi * order * steps / dates
        columns.append(np.cos(angle))
        columns.append(np.sin(angle))
    basis = np.stack(columns, axis=1)
    factor = np.linalg.cholesky(basis.T @ basis)
    return np.linalg.solve(factor.T, np.linalg.solve(factor, basis.T))


def fit_operand(dates, rows):
    wide = np.kron(fit_matrix(dates, TERMS), np.eye(rows)).astype(np.float32)
    high = wide.astype(BF16)
    rest = (wide - high.astype(np.float32)).astype(BF16)
    return np.concatenate([high, rest], axis=0)


def own_order(dates):
    return [0, 1, dates - 2, dates - 1] + list(range(2, dates - 2))


def strip_rows(n, dates):
    q = n >> 3
    date = jnp.where(q < 4 + dates, q - 6, -100)
    date = jnp.where(q < 8, q - 8 + dates, date)
    date = jnp.where(q < 6, q - 4, date)
    date = jnp.where(q < 4, q - 2 + dates, date)
    date = jnp.where(q < 2, q - 2, date)
    return date, n & 7


def halo_rows(m, dates, low, high):
    at = m & (PACK - 1)
    date = jnp.where(at < 2 * (dates + 4), (at >> 1) - 2, -200)
    return date, (at & 1) + jnp.where(m < PACK, low, high)


def kernel(
    sizes,
    refl, mask, time_k, space_k, fit_in,
    filled, coef,
    raw, cloud, fit, chan, packed, gain, out, got, result, smooth_m, select_m,
    in_sem, date_send, date_recv, row_send, row_recv, all_send, all_recv, fill_sem, coef_sem,
):
    nd, nt, dates, bands, rows, cols = sizes
    width = cols // nd
    own = dates * rows
    strip = 4 * rows + own + rows
    total = strip + 2 * PACK
    day = lax.axis_index("date")
    tile = lax.axis_index("tile")
    has_low, has_high = day > 0, day < nd - 1
    has_up, has_down = tile > 0, tile < nt - 1

    def band_in(b):
        return pltpu.make_async_copy(refl.at[:, b], raw.at[b], in_sem.at[b])

    mask_in = pltpu.make_async_copy(mask, cloud, in_sem.at[bands])
    fit_copy = pltpu.make_async_copy(fit_in, fit, in_sem.at[bands + 1])
    mask_in.start()

    @pl.loop(0, bands)
    def _(b):
        band_in(b).start()

    fit_copy.start()

    barrier = pltpu.get_barrier_semaphore()
    for k in range(1, nd):
        pl.semaphore_signal(
            barrier, inc=1, device_id={"date": lax.rem(day + k, nd)}, device_id_type=MESH
        )

    @pl.when(has_up)
    def _():
        pl.semaphore_signal(barrier, inc=1, device_id={"tile": tile - 1}, device_id_type=MESH)

    @pl.when(has_down)
    def _():
        pl.semaphore_signal(barrier, inc=1, device_id={"tile": tile + 1}, device_id_type=MESH)

    at_out = lax.broadcasted_iota(jnp.int32, (own, total), 0)
    at_in = lax.broadcasted_iota(jnp.int32, (own, total), 1)
    q = at_out >> 3
    date_out = jnp.where(q < 2, q, jnp.where(q < 4, q - 4 + dates, q - 2))
    row_out = at_out & 7
    date_a, row_a = strip_rows(at_in, dates)
    date_b, row_b = halo_rows(at_in - strip, dates, -2, rows)
    inside = at_in < strip
    apart = jnp.where(inside, date_a, date_b) - date_out
    below = jnp.where(inside, row_a, row_b) - row_out
    weight_t = jnp.zeros((own, total), F32)
    weight_r = jnp.zeros((own, total), F32)
    for k in range(5):
        weight_t = weight_t + jnp.where(apart == k - 2, time_k[k], 0.0)
        weight_r = weight_r + jnp.where(below == k - 2, space_k[k], 0.0)
    weight = weight_t * weight_r
    weight_hi = weight.astype(BF16).astype(F32)
    smooth_m[...] = jnp.concatenate([weight_hi, weight - weight_hi], axis=0).astype(BF16)

    pick = lax.broadcasted_iota(jnp.int32, (2 * PACK, strip), 0)
    date_p, row_p = halo_rows(pick, dates, rows - 2, 0)
    date_s, row_s = strip_rows(lax.broadcasted_iota(jnp.int32, (2 * PACK, strip), 1), dates)
    hit = jnp.logical_and(date_p == date_s, row_p == row_s)
    select_m[...] = jnp.where(hit, 1.0, 0.0).astype(BF16)

    zero_days = jnp.zeros((2 * rows, cols), BF16)
    zero_rows = jnp.zeros((PACK, cols), BF16)

    @pl.loop(0, bands + 1)
    def _(c):
        @pl.when(jnp.logical_not(has_low))
        def _():
            chan[c, pl.ds(0, 2 * rows)] = zero_days

        @pl.when(jnp.logical_not(has_high))
        def _():
            chan[c, pl.ds(2 * rows, 2 * rows)] = zero_days

        @pl.when(jnp.logical_not(has_up))
        def _():
            chan[c, pl.ds(strip, PACK)] = zero_rows

        @pl.when(jnp.logical_not(has_down))
        def _():
            chan[c, pl.ds(strip + PACK, PACK)] = zero_rows

    def later(c):
        return pltpu.make_async_remote_copy(
            src_ref=chan.at[c, pl.ds(6 * rows, 2 * rows)],
            dst_ref=chan.at[c, pl.ds(0, 2 * rows)],
            send_sem=date_send.at[c, 0],
            recv_sem=date_recv.at[c, 0],
            device_id={"date": jnp.minimum(day + 1, nd - 1)},
            device_id_type=MESH,
        )

    def earlier(c):
        return pltpu.make_async_remote_copy(
            src_ref=chan.at[c, pl.ds(4 * rows, 2 * rows)],
            dst_ref=chan.at[c, pl.ds(2 * rows, 2 * rows)],
            send_sem=date_send.at[c, 1],
            recv_sem=date_recv.at[c, 1],
            device_id={"date": jnp.maximum(day - 1, 0)},
            device_id_type=MESH,
        )

    def downward(c):
        return pltpu.make_async_remote_copy(
            src_ref=packed.at[c, pl.ds(0, PACK)],
            dst_ref=chan.at[c, pl.ds(strip, PACK)],
            send_sem=row_send.at[c, 0],
            recv_sem=row_recv.at[c, 0],
            device_id={"tile": jnp.minimum(tile + 1, nt - 1)},
            device_id_type=MESH,
        )

    def upward(c):
        return pltpu.make_async_remote_copy(
            src_ref=packed.at[c, pl.ds(PACK, PACK)],
            dst_ref=chan.at[c, pl.ds(strip + PACK, PACK)],
            send_sem=row_send.at[c, 1],
            recv_sem=row_recv.at[c, 1],
            device_id={"tile": jnp.maximum(tile - 1, 0)},
            device_id_type=MESH,
        )

    def send_dates(c):
        @pl.when(has_high)
        def _():
            later(c).start()

        @pl.when(has_low)
        def _():
            earlier(c).start()

    blank = jnp.zeros((rows, cols), F32)

    def store_own(c, values):
        parts = [values(t) for t in own_order(dates)] + [blank]
        chan[c, pl.ds(4 * rows, own + rows)] = jnp.concatenate(parts, axis=0).astype(BF16)

    mask_in.wait()
    store_own(0, lambda t: cloud[t].astype(F32))
    pl.semaphore_wait(
        barrier, nd - 1 + jnp.where(has_up, 1, 0) + jnp.where(has_down, 1, 0)
    )
    send_dates(0)

    @pl.loop(0, bands)
    def _(b):
        band_in(b).wait()
        store_own(b + 1, lambda t: raw[b, t].astype(F32) * cloud[t].astype(F32))
        send_dates(b + 1)

    def share_rows(c):
        @pl.when(has_low)
        def _():
            later(c).wait_recv()

        @pl.when(has_high)
        def _():
            earlier(c).wait_recv()

        packed[c] = jnp.dot(
            select_m[...], chan[c, pl.ds(0, strip)], preferred_element_type=F32
        ).astype(BF16)

        @pl.when(has_down)
        def _():
            downward(c).start()

        @pl.when(has_up)
        def _():
            upward(c).start()

    def smoothed(c):
        @pl.when(has_up)
        def _():
            downward(c).wait_recv()

        @pl.when(has_down)
        def _():
            upward(c).wait_recv()

        both = jnp.dot(smooth_m[...], chan[c], preferred_element_type=F32)
        rowed = both[:own] + both[own:]
        rowed = jnp.concatenate([rowed, jnp.zeros((own, 128), F32)], axis=1)
        across = cols + 128
        field = space_k[2] * rowed
        for k in (0, 1, 3, 4):
            field = field + space_k[k] * pltpu.roll(rowed, (2 - k) % across, 1)
        return field[:, :cols]

    def own_part(c):
        return chan[c, pl.ds(4 * rows, own + rows)].astype(F32)[:own]

    def send_to(b, k):
        peer = lax.rem(day + k, nd)
        return pltpu.make_async_remote_copy(
            src_ref=out.at[b, peer],
            dst_ref=got.at[b, day],
            send_sem=all_send.at[b],
            recv_sem=all_recv.at[b],
            device_id={"date": peer},
            device_id_type=MESH,
        )

    def fill_out(b):
        return pltpu.make_async_copy(raw.at[b], filled.at[:, b], fill_sem.at[b])

    def coef_out(c):
        return pltpu.make_async_copy(result.at[c], coef.at[c], coef_sem.at[c])

    def fill_band(b):
        whole = own_part(b + 1) + gain[...] * smoothed(b + 1)
        for q, t in enumerate(own_order(dates)):
            strip_t = whole[q * rows : (q + 1) * rows].astype(BF16)
            raw[b, t] = strip_t
            for j in range(nd):
                out[b, j, t] = strip_t[:, j * width : (j + 1) * width]
        for k in range(1, nd):
            send_to(b, (k + nd // 2 - 1) % (nd - 1) + 1).start()
        pltpu.make_async_copy(out.at[b, day], got.at[b, day], all_recv.at[b]).start()
        fill_out(b).start()

    for c in range(AHEAD):
        share_rows(c)
    gain[...] = (1.0 - own_part(0)) / (smoothed(0) + 1.0)

    @pl.loop(0, bands)
    def _(b):
        @pl.when(b + AHEAD <= bands)
        def _():
            share_rows(b + AHEAD)

        fill_band(b)

    fit_copy.wait()

    def project(c, series):
        flat = series.reshape(nd * dates * rows, width).astype(BF16)
        both = jnp.dot(fit[...], flat, preferred_element_type=F32)
        half = TERMS * rows
        result[c] = (both[:half] + both[half:]).reshape(TERMS, rows, width)
        coef_out(c).start()

    def arrived(b):
        pltpu.make_async_copy(got.at[b], got.at[b], all_recv.at[b]).wait()

    @pl.loop(0, bands - 1)
    def _(b):
        arrived(b)
        project(b, got[b].astype(F32))

    red, near, swir = got[2].astype(F32), got[6].astype(F32), got[8].astype(F32)
    project(bands, 1.5 * (near - red) / (near + red + 0.5))
    project(bands + 1, (near - swir) / (near + swir + 0.5))
    arrived(bands - 1)
    project(bands - 1, got[bands - 1].astype(F32))

    @pl.loop(0, bands + 1)
    def _(c):
        @pl.when(has_high)
        def _():
            later(c).wait_send()

        @pl.when(has_low)
        def _():
            earlier(c).wait_send()

        @pl.when(has_down)
        def _():
            downward(c).wait_send()

        @pl.when(has_up)
        def _():
            upward(c).wait_send()

    @pl.loop(0, bands)
    def _(b):
        fill_out(b).wait()
        sent = out.at[b, pl.ds(0, nd - 1)]
        pltpu.make_async_copy(sent, sent, all_send.at[b]).wait()

    @pl.loop(0, bands + 2)
    def _(c):
        coef_out(c).wait()


def solution(mesh):
    nd, nt = mesh.shape["date"], mesh.shape["tile"]

    def per_device(reflectance, clear_mask, time_kernel, space_kernel):
        dates, bands, rows, cols = reflectance.shape
        width = cols // nd
        own = dates * rows
        strip = 4 * rows + own + rows
        total = strip + 2 * PACK
        whole = nd * own
        anywhere = pl.BlockSpec(memory_space=pl.ANY)
        scalars = pl.BlockSpec(memory_space=pltpu.SMEM)
        dma = pltpu.SemaphoreType.DMA
        return pl.pallas_call(
            functools.partial(kernel, (nd, nt, dates, bands, rows, cols)),
            out_shape=(
                jax.ShapeDtypeStruct((dates, bands, rows, cols), BF16),
                jax.ShapeDtypeStruct((bands + 2, TERMS, rows, width), F32),
            ),
            in_specs=[anywhere, anywhere, scalars, scalars, anywhere],
            out_specs=(anywhere, anywhere),
            scratch_shapes=[
                pltpu.VMEM((bands, dates, rows, cols), BF16),
                pltpu.VMEM((dates, rows, cols), jnp.int32),
                pltpu.VMEM((2 * TERMS * rows, whole), BF16),
                pltpu.VMEM((bands + 1, total, cols), BF16),
                pltpu.VMEM((bands + 1, 2 * PACK, cols), BF16),
                pltpu.VMEM((own, cols), F32),
                pltpu.VMEM((bands, nd, dates, rows, width), BF16),
                pltpu.VMEM((bands, nd, dates, rows, width), BF16),
                pltpu.VMEM((bands + 2, TERMS, rows, width), F32),
                pltpu.VMEM((2 * own, total), BF16),
                pltpu.VMEM((2 * PACK, strip), BF16),
                dma((bands + 2,)),
                dma((bands + 1, 2)),
                dma((bands + 1, 2)),
                dma((bands + 1, 2)),
                dma((bands + 1, 2)),
                dma((bands,)),
                dma((bands,)),
                dma((bands,)),
                dma((bands + 2,)),
            ],
            compiler_params=pltpu.CompilerParams(
                collective_id=0, has_side_effects=True, vmem_limit_bytes=56 * 2**20
            ),
            name="fill_and_fit",
        )(
            reflectance,
            clear_mask,
            time_kernel,
            space_kernel,
            jnp.asarray(fit_operand(nd * dates, rows)),
        )

    placed = (P("date", None, "tile", None), P("date", "tile", None), P(), P())
    return jax.shard_map(
        per_device,
        mesh=mesh,
        in_specs=placed,
        out_specs=(P("date", None, "tile", None), P(None, None, "tile", "date")),
        check_vma=False,
    )
```

time: 295 us -> 115 us (0.39)
  the two profiles are of different devices: /device:TPU:8 before, /device:TPU:480 now
where the time goes in v1:
time: 115 us
  Pallas kernels  110 us (96%)
  local copies, waits for them, and re-layouts  3.7 us (3%)
    pallas_call x1, Pallas kernels, per_device(): pl.pallas_call(functools.partial(kernel, (nd, nt, dates, bands, rows, col...  110 us
    unnamed x4, local copies, waits for them, and re-layouts  3.7 us

profile of v1, /device:TPU:480, one launch (start us, length us, event | category | flops | bytes accessed | tf_op | source)
XLA Modules:
  0.0 114.6 jit_solution(15055370946729015364)
XLA Ops:
  0.6 110.3 %fill_and_fit.1 = (bf16[9,10,8,1024]{3,2,1,0:T(8,128)(2,1)}, f32[12,24,8,128]{3,2,1,0:T(8,128)}) custom-call(bf16[9,10,8,1024]{3,2,1,0:T(8,128)(2,1)} %refl.1, s32[9,8,1024]{2,1,0:T(8,128)} %mask.1, f32[5]{0:T(128)} %time_k.1, f32[5]{0:T(128)} %space_k.1, bf16[384,576]{1,0:T(8,128)(2,1)} %constant.2.clone.fit_in), custom_call_target="tpu_custom_call" | custom-call | tf_op jit(solution)/shard_map/fill_and_fit/pallas_call | solution.py:365
  110.9 0.0 copy-start
  110.9 2.7 %copy.9 = bf16[9,10,8,1024]{3,2,1,0:T(8,128)(2,1)} copy(bf16[9,10,8,1024]{3,2,1,0:T(8,128)(2,1)} %get-tuple-element.4) | data formatting | bytes 2949120
  113.6 0.0 copy-done
  113.6 1.0 copy.10
Async XLA Ops:
  110.9 2.7 %copy-start = (f32[12,24,8,128]{3,2,1,0:T(8,128)S(1)}, f32[12,24,8,128]{3,2,1,0:T(8,128)}, u32[]{:S(2)}) copy-start(f32[12,24,8,128]{3,2,1,0:T(8,128)} %get-tuple-element.5) | copy-start | bytes 3538948

commit v2 on v1

--- a/solution.py
+++ b/solution.py
@@ -56,12 +56,17 @@
     return date, (at & 1) + jnp.where(m < PACK, low, high)
 
 
+def relay(c, way, half, channels):
+    return 2 * (c + 1) + way if half >= 2 * (channels + 2) else 1
+
+
 def kernel(
     sizes,
     refl, mask, time_k, space_k, fit_in,
     filled, coef,
-    raw, cloud, fit, chan, packed, gain, out, got, result, smooth_m, select_m,
-    in_sem, date_send, date_recv, row_send, row_recv, all_send, all_recv, fill_sem, coef_sem,
+    raw, cloud, fit, chan, packed, hold, gain, out, got, result, smooth_m, select_m,
+    in_sem, date_send, date_recv, row_send, row_recv, hop_send, hop_recv,
+    all_send, all_recv, fill_sem, coef_sem,
 ):
     nd, nt, dates, bands, rows, cols = sizes
     width = cols // nd
@@ -72,33 +77,147 @@
     tile = lax.axis_index("tile")
     has_low, has_high = day > 0, day < nd - 1
     has_up, has_down = tile > 0, tile < nt - 1
+    half = nt // 2
+    ends_low, ends_high = tile == half - 1, tile == half
+    channels = bands + 1
+
+    def passes(c, way):
+        return tile == (half if way else 0) + relay(c, way, half, channels)
 
     def band_in(b):
         return pltpu.make_async_copy(refl.at[:, b], raw.at[b], in_sem.at[b])
 
     mask_in = pltpu.make_async_copy(mask, cloud, in_sem.at[bands])
     fit_copy = pltpu.make_async_copy(fit_in, fit, in_sem.at[bands + 1])
-    mask_in.start()
-
-    @pl.loop(0, bands)
-    def _(b):
-        band_in(b).start()
-
-    fit_copy.start()
-
     barrier = pltpu.get_barrier_semaphore()
     for k in range(1, nd):
         pl.semaphore_signal(
             barrier, inc=1, device_id={"date": lax.rem(day + k, nd)}, device_id_type=MESH
         )
 
-    @pl.when(has_up)
-    def _():
-        pl.semaphore_signal(barrier, inc=1, device_id={"tile": tile - 1}, device_id_type=MESH)
-
-    @pl.when(has_down)
-    def _():
-        pl.semaphore_signal(barrier, inc=1, device_id={"tile": tile + 1}, device_id_type=MESH)
+    def greet(strip):
+        pl.semaphore_signal(barrier, inc=1, device_id={"tile": strip}, device_id_type=MESH)
+
+    mask_in.start()
+
+    @pl.loop(0, bands)
+    def _(b):
+        band_in(b).start()
+
+    fit_copy.start()
+
+    pl.when(has_up)(lambda: greet(tile - 1))
+    pl.when(has_down)(lambda: greet(tile + 1))
+    greeted = jnp.where(has_up, 1, 0) + jnp.where(has_down, 1, 0)
+    greeted = greeted + jnp.where(jnp.logical_or(ends_low, ends_high), bands, 0)
+
+    @pl.loop(1, channels)
+    def _(c):
+        for way in (0, 1):
+            at = (half if way else 0) + relay(c, way, half, channels)
+            pl.when(passes(c, way))(lambda: greet(half if way else half - 1))
+            pl.when(ends_low if way else ends_high)(lambda: greet(at))
+
+    for way in (0, 1):
+
+        def count(c, total):
+            return total + jnp.where(passes(c, way), 1, 0)
+
+        greeted = lax.fori_loop(1, channels, count, greeted)
+
+    def later(c):
+        return pltpu.make_async_remote_copy(
+            src_ref=chan.at[c, pl.ds(6 * rows, 2 * rows)],
+            dst_ref=chan.at[c, pl.ds(0, 2 * rows)],
+            send_sem=date_send.at[c, 0],
+            recv_sem=date_recv.at[c, 0],
+            device_id={"date": jnp.minimum(day + 1, nd - 1)},
+            device_id_type=MESH,
+        )
+
+    def earlier(c):
+        return pltpu.make_async_remote_copy(
+            src_ref=chan.at[c, pl.ds(4 * rows, 2 * rows)],
+            dst_ref=chan.at[c, pl.ds(2 * rows, 2 * rows)],
+            send_sem=date_send.at[c, 1],
+            recv_sem=date_recv.at[c, 1],
+            device_id={"date": jnp.maximum(day - 1, 0)},
+            device_id_type=MESH,
+        )
+
+    def downward(c):
+        return pltpu.make_async_remote_copy(
+            src_ref=packed.at[c, pl.ds(0, PACK)],
+            dst_ref=chan.at[c, pl.ds(strip, PACK)],
+            send_sem=row_send.at[c, 0],
+            recv_sem=row_recv.at[c, 0],
+            device_id={"tile": jnp.minimum(tile + 1, nt - 1)},
+            device_id_type=MESH,
+        )
+
+    def upward(c):
+        return pltpu.make_async_remote_copy(
+            src_ref=packed.at[c, pl.ds(PACK, PACK)],
+            dst_ref=chan.at[c, pl.ds(strip + PACK, PACK)],
+            send_sem=row_send.at[c, 1],
+            recv_sem=row_recv.at[c, 1],
+            device_id={"tile": jnp.maximum(tile - 1, 0)},
+            device_id_type=MESH,
+        )
+
+    def depart(c, way):
+        return pltpu.make_async_remote_copy(
+            src_ref=packed.at[c, pl.ds(way * PACK, PACK)],
+            dst_ref=hold.at[way, c],
+            send_sem=row_send.at[c, way],
+            recv_sem=hop_recv.at[way, c],
+            device_id={"tile": (half if way else 0) + relay(c, way, half, channels)},
+            device_id_type=MESH,
+        )
+
+    def arrive(c, way):
+        return pltpu.make_async_remote_copy(
+            src_ref=hold.at[way, c],
+            dst_ref=chan.at[c, pl.ds(strip + way * PACK, PACK)],
+            send_sem=hop_send.at[way, c],
+            recv_sem=row_recv.at[c, way],
+            device_id={"tile": half - 1 if way else half},
+            device_id_type=MESH,
+        )
+
+    def pass_on(c):
+        for way in (0, 1):
+
+            @pl.when(passes(c, way))
+            def _():
+                depart(c, way).wait_recv()
+                arrive(c, way).start()
+
+    def send_dates(c):
+        @pl.when(has_high)
+        def _():
+            later(c).start()
+
+        @pl.when(has_low)
+        def _():
+            earlier(c).start()
+
+    blank = jnp.zeros((rows, cols), F32)
+
+    def store_own(c, values):
+        parts = [values(t) for t in own_order(dates)] + [blank]
+        chan[c, pl.ds(4 * rows, own + rows)] = jnp.concatenate(parts, axis=0).astype(BF16)
+
+    mask_in.wait()
+    store_own(0, lambda t: cloud[t].astype(F32))
+    pl.semaphore_wait(barrier, nd - 1 + greeted)
+    send_dates(0)
+
+    @pl.loop(0, bands)
+    def _(b):
+        band_in(b).wait()
+        store_own(b + 1, lambda t: raw[b, t].astype(F32) * cloud[t].astype(F32))
+        send_dates(b + 1)
 
     at_out = lax.broadcasted_iota(jnp.int32, (own, total), 0)
     at_in = lax.broadcasted_iota(jnp.int32, (own, total), 1)
@@ -146,74 +265,6 @@
         def _():
             chan[c, pl.ds(strip + PACK, PACK)] = zero_rows
 
-    def later(c):
-        return pltpu.make_async_remote_copy(
-            src_ref=chan.at[c, pl.ds(6 * rows, 2 * rows)],
-            dst_ref=chan.at[c, pl.ds(0, 2 * rows)],
-            send_sem=date_send.at[c, 0],
-            recv_sem=date_recv.at[c, 0],
-            device_id={"date": jnp.minimum(day + 1, nd - 1)},
-            device_id_type=MESH,
-        )
-
-    def earlier(c):
-        return pltpu.make_async_remote_copy(
-            src_ref=chan.at[c, pl.ds(4 * rows, 2 * rows)],
-            dst_ref=chan.at[c, pl.ds(2 * rows, 2 * rows)],
-            send_sem=date_send.at[c, 1],
-            recv_sem=date_recv.at[c, 1],
-            device_id={"date": jnp.maximum(day - 1, 0)},
-            device_id_type=MESH,
-        )
-
-    def downward(c):
-        return pltpu.make_async_remote_copy(
-            src_ref=packed.at[c, pl.ds(0, PACK)],
-            dst_ref=chan.at[c, pl.ds(strip, PACK)],
-            send_sem=row_send.at[c, 0],
-            recv_sem=row_recv.at[c, 0],
-            device_id={"tile": jnp.minimum(tile + 1, nt - 1)},
-            device_id_type=MESH,
-        )
-
-    def upward(c):
-        return pltpu.make_async_remote_copy(
-            src_ref=packed.at[c, pl.ds(PACK, PACK)],
-            dst_ref=chan.at[c, pl.ds(strip + PACK, PACK)],
-            send_sem=row_send.at[c, 1],
-            recv_sem=row_recv.at[c, 1],
-            device_id={"tile": jnp.maximum(tile - 1, 0)},
-            device_id_type=MESH,
-        )
-
-    def send_dates(c):
-        @pl.when(has_high)
-        def _():
-            later(c).start()
-
-        @pl.when(has_low)
-        def _():
-            earlier(c).start()
-
-    blank = jnp.zeros((rows, cols), F32)
-
-    def store_own(c, values):
-        parts = [values(t) for t in own_order(dates)] + [blank]
-        chan[c, pl.ds(4 * rows, own + rows)] = jnp.concatenate(parts, axis=0).astype(BF16)
-
-    mask_in.wait()
-    store_own(0, lambda t: cloud[t].astype(F32))
-    pl.semaphore_wait(
-        barrier, nd - 1 + jnp.where(has_up, 1, 0) + jnp.where(has_down, 1, 0)
-    )
-    send_dates(0)
-
-    @pl.loop(0, bands)
-    def _(b):
-        band_in(b).wait()
-        store_own(b + 1, lambda t: raw[b, t].astype(F32) * cloud[t].astype(F32))
-        send_dates(b + 1)
-
     def share_rows(c):
         @pl.when(has_low)
         def _():
@@ -227,13 +278,12 @@
             select_m[...], chan[c, pl.ds(0, strip)], preferred_element_type=F32
         ).astype(BF16)
 
-        @pl.when(has_down)
-        def _():
-            downward(c).start()
-
-        @pl.when(has_up)
-        def _():
-            upward(c).start()
+        far = c > 0
+        by_relay = jnp.logical_and(ends_low, far), jnp.logical_and(ends_high, far)
+        pl.when(jnp.logical_and(has_down, jnp.logical_not(by_relay[0])))(lambda: downward(c).start())
+        pl.when(jnp.logical_and(has_up, jnp.logical_not(by_relay[1])))(lambda: upward(c).start())
+        pl.when(by_relay[0])(lambda: depart(c, 0).start())
+        pl.when(by_relay[1])(lambda: depart(c, 1).start())
 
     def smoothed(c):
         @pl.when(has_up)
@@ -280,13 +330,16 @@
             raw[b, t] = strip_t
             for j in range(nd):
                 out[b, j, t] = strip_t[:, j * width : (j + 1) * width]
-        for k in range(1, nd):
-            send_to(b, (k + nd // 2 - 1) % (nd - 1) + 1).start()
+        for k in sorted(range(1, nd), key=lambda k: abs(2 * k - nd)):
+            send_to(b, k).start()
         pltpu.make_async_copy(out.at[b, day], got.at[b, day], all_recv.at[b]).start()
         fill_out(b).start()
 
     for c in range(AHEAD):
         share_rows(c)
+        if c >= 2:
+            pass_on(c - 1)
+
     gain[...] = (1.0 - own_part(0)) / (smoothed(0) + 1.0)
 
     @pl.loop(0, bands)
@@ -294,6 +347,10 @@
         @pl.when(b + AHEAD <= bands)
         def _():
             share_rows(b + AHEAD)
+
+        @pl.when(b + AHEAD - 1 <= bands)
+        def _():
+            pass_on(b + AHEAD - 1)
 
         fill_band(b)
 
@@ -330,13 +387,13 @@
         def _():
             earlier(c).wait_send()
 
-        @pl.when(has_down)
-        def _():
-            downward(c).wait_send()
-
-        @pl.when(has_up)
-        def _():
-            upward(c).wait_send()
+        pl.when(has_down)(lambda: downward(c).wait_send())
+        pl.when(has_up)(lambda: upward(c).wait_send())
+
+    @pl.loop(1, channels)
+    def _(c):
+        for way in (0, 1):
+            pl.when(passes(c, way))(lambda: arrive(c, way).wait_send())
 
     @pl.loop(0, bands)
     def _(b):
@@ -347,6 +404,30 @@
     @pl.loop(0, bands + 2)
     def _(c):
         coef_out(c).wait()
+
+
+def hand_over(filled_in, coef_in, filled, coef, fill_at, coef_at, fill_sem, coef_sem):
+    steps = []
+    for source, at, target, sem in (
+        (filled_in, fill_at, filled, fill_sem),
+        (coef_in, coef_at, coef, coef_sem),
+    ):
+        size = source.shape[0] // 3
+        steps += [(source, at, target, sem, i, pl.ds(i * size, size)) for i in range(3)]
+
+    def load(source, at, _, sem, i, part):
+        return pltpu.make_async_copy(source.at[part], at.at[part], sem.at[0, i])
+
+    def store(_, at, target, sem, i, part):
+        return pltpu.make_async_copy(at.at[part], target.at[part], sem.at[1, i])
+
+    for step in steps:
+        load(*step).start()
+    for step in steps:
+        load(*step).wait()
+        store(*step).start()
+    for step in steps:
+        store(*step).wait()
 
 
 def solution(mesh):
@@ -362,12 +443,13 @@
         anywhere = pl.BlockSpec(memory_space=pl.ANY)
         scalars = pl.BlockSpec(memory_space=pltpu.SMEM)
         dma = pltpu.SemaphoreType.DMA
-        return pl.pallas_call(
+        shapes = (
+            jax.ShapeDtypeStruct((dates, bands, rows, cols), BF16),
+            jax.ShapeDtypeStruct((bands + 2, TERMS, rows, width), F32),
+        )
+        results = pl.pallas_call(
             functools.partial(kernel, (nd, nt, dates, bands, rows, cols)),
-            out_shape=(
-                jax.ShapeDtypeStruct((dates, bands, rows, cols), BF16),
-                jax.ShapeDtypeStruct((bands + 2, TERMS, rows, width), F32),
-            ),
+            out_shape=shapes,
             in_specs=[anywhere, anywhere, scalars, scalars, anywhere],
             out_specs=(anywhere, anywhere),
             scratch_shapes=[
@@ -376,6 +458,7 @@
                 pltpu.VMEM((2 * TERMS * rows, whole), BF16),
                 pltpu.VMEM((bands + 1, total, cols), BF16),
                 pltpu.VMEM((bands + 1, 2 * PACK, cols), BF16),
+                pltpu.VMEM((2, bands + 1, PACK, cols), BF16),
                 pltpu.VMEM((own, cols), F32),
                 pltpu.VMEM((bands, nd, dates, rows, width), BF16),
                 pltpu.VMEM((bands, nd, dates, rows, width), BF16),
@@ -387,6 +470,8 @@
                 dma((bands + 1, 2)),
                 dma((bands + 1, 2)),
                 dma((bands + 1, 2)),
+                dma((2, bands + 1)),
+                dma((2, bands + 1)),
                 dma((bands,)),
                 dma((bands,)),
                 dma((bands,)),
@@ -403,6 +488,20 @@
             space_kernel,
             jnp.asarray(fit_operand(nd * dates, rows)),
         )
+        return pl.pallas_call(
+            hand_over,
+            out_shape=shapes,
+            in_specs=[anywhere, anywhere],
+            out_specs=(anywhere, anywhere),
+            scratch_shapes=[
+                pltpu.VMEM((dates, bands, rows, cols), BF16),
+                pltpu.VMEM((bands + 2, TERMS, rows, width), F32),
+                dma((2, 3)),
+                dma((2, 3)),
+            ],
+            compiler_params=pltpu.CompilerParams(vmem_limit_bytes=60 * 2**20),
+            name="hand_over",
+        )(*results)
 
     placed = (P("date", None, "tile", None), P("date", "tile", None), P(), P())
     return jax.shard_map(

time: 115 us -> 98.5 us (0.86)
  the two profiles are of different devices: /device:TPU:480 before, /device:TPU:8 now
where the time goes in v2:
time: 98.5 us; the launch traced here: 98.3 us
  Pallas kernels  97.7 us (99%)
    pallas_call x1, Pallas kernels, per_device(): pl.pallas_call(functools.partial(kernel, (nd, nt, dates, bands, rows, col...  94.8 us
    pallas_call x1, Pallas kernels, per_device(): pl.pallas_call(hand_over, out_shape=shapes, in_specs=[anywhere, anywhere]...  2.83 us

profile of v2, /device:TPU:8, one launch (start us, length us, event | category | flops | bytes accessed | tf_op | source)
XLA Modules:
  0.0 98.3 jit_solution(16790384379591877949)
XLA Ops:
  0.6 94.8 %fill_and_fit.1 = (bf16[9,10,8,1024]{3,2,1,0:T(8,128)(2,1)}, f32[12,24,8,128]{3,2,1,0:T(8,128)}) custom-call(bf16[9,10,8,1024]{3,2,1,0:T(8,128)(2,1)} %refl.1, s32[9,8,1024]{2,1,0:T(8,128)} %mask.1, f32[5]{0:T(128)} %time_k.1, f32[5]{0:T(128)} %space_k.1, bf16[384,576]{1,0:T(8,128)(2,1)} %constant.2.clone.fit_in), custom_call_target="tpu_custom_call" | custom-call | tf_op jit(solution)/shard_map/fill_and_fit/pallas_call | solution.py:450
  95.5 2.8 %hand_over.1 = (bf16[9,10,8,1024]{3,2,1,0:T(8,128)(2,1)}, f32[12,24,8,128]{3,2,1,0:T(8,128)}) custom-call(bf16[9,10,8,1024]{3,2,1,0:T(8,128)(2,1)} %get-tuple-element.4.filled_in, f32[12,24,8,128]{3,2,1,0:T(8,128)} %get-tuple-element.5.coef_in), custom_call_target="tpu_custom_call" | custom-call | tf_op jit(solution)/shard_map/hand_over/pallas_call | solution.py:491

commit v3 on v2

--- a/solution.py
+++ b/solution.py
@@ -64,9 +64,9 @@
     sizes,
     refl, mask, time_k, space_k, fit_in,
     filled, coef,
-    raw, cloud, fit, chan, packed, hold, gain, out, got, result, smooth_m, select_m,
+    raw, cloud, fit, chan, packed, hold, gain, out, got, smooth_m, select_m,
     in_sem, date_send, date_recv, row_send, row_recv, hop_send, hop_recv,
-    all_send, all_recv, fill_sem, coef_sem,
+    all_send, all_recv, ready,
 ):
     nd, nt, dates, bands, rows, cols = sizes
     width = cols // nd
@@ -106,24 +106,29 @@
 
     fit_copy.start()
 
-    pl.when(has_up)(lambda: greet(tile - 1))
+    pl.when(jnp.logical_and(has_up, tile != half))(lambda: greet(tile - 1))
     pl.when(has_down)(lambda: greet(tile + 1))
-    greeted = jnp.where(has_up, 1, 0) + jnp.where(has_down, 1, 0)
-    greeted = greeted + jnp.where(jnp.logical_or(ends_low, ends_high), bands, 0)
+    greeted = jnp.where(has_up, 1, 0)
+    greeted = greeted + jnp.where(jnp.logical_and(has_down, tile != half - 1), 1, 0)
+    greeted = greeted + jnp.where(ends_low, bands, 0) + jnp.where(ends_high, 2 * bands, 0)
 
     @pl.loop(1, channels)
     def _(c):
-        for way in (0, 1):
-            at = (half if way else 0) + relay(c, way, half, channels)
-            pl.when(passes(c, way))(lambda: greet(half if way else half - 1))
-            pl.when(ends_low if way else ends_high)(lambda: greet(at))
-
-    for way in (0, 1):
-
-        def count(c, total):
-            return total + jnp.where(passes(c, way), 1, 0)
-
-        greeted = lax.fori_loop(1, channels, count, greeted)
+        @pl.when(passes(c, 0))
+        def _():
+            greet(half - 1)
+            greet(half)
+
+        pl.when(passes(c, 1))(lambda: greet(half))
+        pl.when(ends_low)(lambda: greet(half + relay(c, 1, half, channels)))
+
+    def count(c, total):
+        return total + jnp.where(passes(c, 1), 1, 0)
+
+    greeted = lax.fori_loop(1, channels, count, greeted)
+
+    def tell_ready(strip):
+        pl.semaphore_signal(ready, inc=1, device_id={"tile": strip}, device_id_type=MESH)
 
     def later(c):
         return pltpu.make_async_remote_copy(
@@ -185,13 +190,13 @@
             device_id_type=MESH,
         )
 
-    def pass_on(c):
-        for way in (0, 1):
-
-            @pl.when(passes(c, way))
-            def _():
-                depart(c, way).wait_recv()
-                arrive(c, way).start()
+    def pass_on(c, way):
+        @pl.when(passes(c, way))
+        def _():
+            depart(c, way).wait_recv()
+            if way == 0:
+                pl.semaphore_wait(ready, 1)
+            arrive(c, way).start()
 
     def send_dates(c):
         @pl.when(has_high)
@@ -211,6 +216,15 @@
     mask_in.wait()
     store_own(0, lambda t: cloud[t].astype(F32))
     pl.semaphore_wait(barrier, nd - 1 + greeted)
+
+    @pl.when(ends_high)
+    def _():
+        tell_ready(half - 1)
+
+        @pl.loop(1, channels)
+        def _(c):
+            tell_ready(relay(c, 0, half, channels))
+
     send_dates(0)
 
     @pl.loop(0, bands)
@@ -279,6 +293,7 @@
         ).astype(BF16)
 
         far = c > 0
+        pl.when(jnp.logical_and(ends_low, c == 0))(lambda: pl.semaphore_wait(ready, 1))
         by_relay = jnp.logical_and(ends_low, far), jnp.logical_and(ends_high, far)
         pl.when(jnp.logical_and(has_down, jnp.logical_not(by_relay[0])))(lambda: downward(c).start())
         pl.when(jnp.logical_and(has_up, jnp.logical_not(by_relay[1])))(lambda: upward(c).start())
@@ -317,65 +332,84 @@
             device_id_type=MESH,
         )
 
-    def fill_out(b):
-        return pltpu.make_async_copy(raw.at[b], filled.at[:, b], fill_sem.at[b])
-
-    def coef_out(c):
-        return pltpu.make_async_copy(result.at[c], coef.at[c], coef_sem.at[c])
-
     def fill_band(b):
         whole = own_part(b + 1) + gain[...] * smoothed(b + 1)
         for q, t in enumerate(own_order(dates)):
             strip_t = whole[q * rows : (q + 1) * rows].astype(BF16)
-            raw[b, t] = strip_t
+            filled[t, b] = strip_t
             for j in range(nd):
                 out[b, j, t] = strip_t[:, j * width : (j + 1) * width]
-        for k in sorted(range(1, nd), key=lambda k: abs(2 * k - nd)):
+        for k in (4, 3, 5):
             send_to(b, k).start()
         pltpu.make_async_copy(out.at[b, day], got.at[b, day], all_recv.at[b]).start()
-        fill_out(b).start()
 
     for c in range(AHEAD):
         share_rows(c)
         if c >= 2:
-            pass_on(c - 1)
+            pass_on(c - 1, 1)
+
+    pass_on(AHEAD - 1, 1)
+    pass_on(AHEAD, 1)
+
+    at_gap = jnp.logical_or(ends_low, ends_high)
+
+    @pl.when(at_gap)
+    def _():
+        @pl.loop(AHEAD, channels)
+        def _(c):
+            share_rows(c)
 
     gain[...] = (1.0 - own_part(0)) / (smoothed(0) + 1.0)
 
     @pl.loop(0, bands)
     def _(b):
-        @pl.when(b + AHEAD <= bands)
+        @pl.when(jnp.logical_and(b + AHEAD <= bands, jnp.logical_not(at_gap)))
         def _():
             share_rows(b + AHEAD)
 
-        @pl.when(b + AHEAD - 1 <= bands)
-        def _():
-            pass_on(b + AHEAD - 1)
-
+        pl.when(b + AHEAD + 1 <= bands)(lambda: pass_on(b + AHEAD + 1, 1))
         fill_band(b)
 
+        @pl.when(b < 3)
+        def _():
+            pass_on(2 * b + 1, 0)
+            pass_on(2 * b + 2, 0)
+
+        pl.when(jnp.logical_and(b >= 3, b + 4 <= bands))(lambda: pass_on(b + 4, 0))
+
+    for k in (2, 1, 6, 7):
+        @pl.loop(0, bands)
+        def _(b):
+            send_to(b, k).start()
+
     fit_copy.wait()
 
-    def project(c, series):
-        flat = series.reshape(nd * dates * rows, width).astype(BF16)
-        both = jnp.dot(fit[...], flat, preferred_element_type=F32)
-        half = TERMS * rows
-        result[c] = (both[:half] + both[half:]).reshape(TERMS, rows, width)
-        coef_out(c).start()
+    def project(places, pair):
+        flat = [x.reshape(nd * dates * rows, width).astype(BF16) for x in pair]
+        both = jnp.dot(fit[...], jnp.concatenate(flat, axis=1), preferred_element_type=F32)
+        middle = TERMS * rows
+        terms = both[:middle] + both[middle:]
+        for i, c in enumerate(places):
+            coef[c] = terms[:, i * width : (i + 1) * width].reshape(TERMS, rows, width)
 
     def arrived(b):
         pltpu.make_async_copy(got.at[b], got.at[b], all_recv.at[b]).wait()
 
-    @pl.loop(0, bands - 1)
-    def _(b):
-        arrived(b)
-        project(b, got[b].astype(F32))
-
-    red, near, swir = got[2].astype(F32), got[6].astype(F32), got[8].astype(F32)
-    project(bands, 1.5 * (near - red) / (near + red + 0.5))
-    project(bands + 1, (near - swir) / (near + swir + 0.5))
+    def series(b):
+        return got[b].astype(F32)
+
+    @pl.loop(0, bands // 2 - 1)
+    def _(i):
+        arrived(2 * i)
+        arrived(2 * i + 1)
+        project((2 * i, 2 * i + 1), (series(2 * i), series(2 * i + 1)))
+
+    arrived(bands - 2)
+    red, near, swir = series(2), series(6), series(8)
+    savi = 1.5 * (near - red) / (near + red + 0.5)
+    project((bands, bands + 1), (savi, (near - swir) / (near + swir + 0.5)))
     arrived(bands - 1)
-    project(bands - 1, got[bands - 1].astype(F32))
+    project((bands - 2, bands - 1), (series(bands - 2), series(bands - 1)))
 
     @pl.loop(0, bands + 1)
     def _(c):
@@ -397,37 +431,8 @@
 
     @pl.loop(0, bands)
     def _(b):
-        fill_out(b).wait()
         sent = out.at[b, pl.ds(0, nd - 1)]
         pltpu.make_async_copy(sent, sent, all_send.at[b]).wait()
-
-    @pl.loop(0, bands + 2)
-    def _(c):
-        coef_out(c).wait()
-
-
-def hand_over(filled_in, coef_in, filled, coef, fill_at, coef_at, fill_sem, coef_sem):
-    steps = []
-    for source, at, target, sem in (
-        (filled_in, fill_at, filled, fill_sem),
-        (coef_in, coef_at, coef, coef_sem),
-    ):
-        size = source.shape[0] // 3
-        steps += [(source, at, target, sem, i, pl.ds(i * size, size)) for i in range(3)]
-
-    def load(source, at, _, sem, i, part):
-        return pltpu.make_async_copy(source.at[part], at.at[part], sem.at[0, i])
-
-    def store(_, at, target, sem, i, part):
-        return pltpu.make_async_copy(at.at[part], target.at[part], sem.at[1, i])
-
-    for step in steps:
-        load(*step).start()
-    for step in steps:
-        load(*step).wait()
-        store(*step).start()
-    for step in steps:
-        store(*step).wait()
 
 
 def solution(mesh):
@@ -441,17 +446,18 @@
         total = strip + 2 * PACK
         whole = nd * own
         anywhere = pl.BlockSpec(memory_space=pl.ANY)
+        inside = pl.BlockSpec(memory_space=pltpu.VMEM)
         scalars = pl.BlockSpec(memory_space=pltpu.SMEM)
         dma = pltpu.SemaphoreType.DMA
         shapes = (
             jax.ShapeDtypeStruct((dates, bands, rows, cols), BF16),
             jax.ShapeDtypeStruct((bands + 2, TERMS, rows, width), F32),
         )
-        results = pl.pallas_call(
+        return pl.pallas_call(
             functools.partial(kernel, (nd, nt, dates, bands, rows, cols)),
-            out_shape=shapes,
+            out_shape=tuple(pltpu.VMEM(s.shape, s.dtype) for s in shapes),
             in_specs=[anywhere, anywhere, scalars, scalars, anywhere],
-            out_specs=(anywhere, anywhere),
+            out_specs=(inside, inside),
             scratch_shapes=[
                 pltpu.VMEM((bands, dates, rows, cols), BF16),
                 pltpu.VMEM((dates, rows, cols), jnp.int32),
@@ -462,7 +468,6 @@
                 pltpu.VMEM((own, cols), F32),
                 pltpu.VMEM((bands, nd, dates, rows, width), BF16),
                 pltpu.VMEM((bands, nd, dates, rows, width), BF16),
-                pltpu.VMEM((bands + 2, TERMS, rows, width), F32),
                 pltpu.VMEM((2 * own, total), BF16),
                 pltpu.VMEM((2 * PACK, strip), BF16),
                 dma((bands + 2,)),
@@ -474,8 +479,7 @@
                 dma((2, bands + 1)),
                 dma((bands,)),
                 dma((bands,)),
-                dma((bands,)),
-                dma((bands + 2,)),
+                pltpu.SemaphoreType.REGULAR,
             ],
             compiler_params=pltpu.CompilerParams(
                 collective_id=0, has_side_effects=True, vmem_limit_bytes=56 * 2**20
@@ -488,20 +492,6 @@
             space_kernel,
             jnp.asarray(fit_operand(nd * dates, rows)),
         )
-        return pl.pallas_call(
-            hand_over,
-            out_shape=shapes,
-            in_specs=[anywhere, anywhere],
-            out_specs=(anywhere, anywhere),
-            scratch_shapes=[
-                pltpu.VMEM((dates, bands, rows, cols), BF16),
-                pltpu.VMEM((bands + 2, TERMS, rows, width), F32),
-                dma((2, 3)),
-                dma((2, 3)),
-            ],
-            compiler_params=pltpu.CompilerParams(vmem_limit_bytes=60 * 2**20),
-            name="hand_over",
-        )(*results)
 
     placed = (P("date", None, "tile", None), P("date", "tile", None), P(), P())
     return jax.shard_map(

time: 98.5 us -> 94 us (0.954)
  the two profiles are of different devices: /device:TPU:8 before, /device:TPU:127 now
where the time goes in v3:
time: 94 us; the launch traced here: 93.9 us
  Pallas kernels  91.1 us (97%)
  local copies, waits for them, and re-layouts  2.13 us (2%)
    pallas_call x1, Pallas kernels, per_device(): pl.pallas_call(functools.partial(kernel, (nd, nt, dates, bands, rows, col...  91.1 us
    unnamed x2, local copies, waits for them, and re-layouts  2.13 us

profile of v3, /device:TPU:127, one launch (start us, length us, event | category | flops | bytes accessed | tf_op | source)
XLA Modules:
  0.0 93.9 jit_solution(5189495990684562969)
XLA Ops:
  0.6 91.1 %fill_and_fit.1 = (bf16[9,10,8,1024]{3,2,1,0:T(8,128)(2,1)S(1)}, f32[12,24,8,128]{3,2,1,0:T(8,128)S(1)}) custom-call(bf16[9,10,8,1024]{3,2,1,0:T(8,128)(2,1)} %refl.1, s32[9,8,1024]{2,1,0:T(8,128)} %mask.1, f32[5]{0:T(128)} %time_k.1, f32[5]{0:T(128)} %space_k.1, bf16[384,576]{1,0:T(8,128)(2,1)} %constant.2.clone.fit_in), custom_call_target="tpu_custom_call" | custom-call | tf_op jit(solution)/shard_map/fill_and_fit/pallas_call | solution.py:456
  91.7 1.1 %copy.9 = bf16[9,10,8,1024]{3,2,1,0:T(8,128)(2,1)} copy(bf16[9,10,8,1024]{3,2,1,0:T(8,128)(2,1)S(1)} %get-tuple-element.2) | data formatting | bytes 2949120
  92.8 1.0 %copy.10 = f32[12,24,8,128]{3,2,1,0:T(8,128)} copy(f32[12,24,8,128]{3,2,1,0:T(8,128)S(1)} %get-tuple-element.3) | data formatting | bytes 2359296

commit v4 on v3

--- a/solution.py
+++ b/solution.py
@@ -293,9 +293,8 @@
         ).astype(BF16)
 
         far = c > 0
-        pl.when(jnp.logical_and(ends_low, c == 0))(lambda: pl.semaphore_wait(ready, 1))
         by_relay = jnp.logical_and(ends_low, far), jnp.logical_and(ends_high, far)
-        pl.when(jnp.logical_and(has_down, jnp.logical_not(by_relay[0])))(lambda: downward(c).start())
+        pl.when(jnp.logical_and(has_down, jnp.logical_not(ends_low)))(lambda: downward(c).start())
         pl.when(jnp.logical_and(has_up, jnp.logical_not(by_relay[1])))(lambda: upward(c).start())
         pl.when(by_relay[0])(lambda: depart(c, 0).start())
         pl.when(by_relay[1])(lambda: depart(c, 1).start())
@@ -353,12 +352,18 @@
 
     at_gap = jnp.logical_or(ends_low, ends_high)
 
+    @pl.when(ends_low)
+    def _():
+        pl.semaphore_wait(ready, 1)
+        downward(0).start()
+
     @pl.when(at_gap)
     def _():
         @pl.loop(AHEAD, channels)
         def _(c):
             share_rows(c)
 
+
     gain[...] = (1.0 - own_part(0)) / (smoothed(0) + 1.0)
 
     @pl.loop(0, bands)
@@ -367,7 +372,12 @@
         def _():
             share_rows(b + AHEAD)
 
-        pl.when(b + AHEAD + 1 <= bands)(lambda: pass_on(b + AHEAD + 1, 1))
+
+        @pl.when(2 * b + AHEAD + 2 <= bands)
+        def _():
+            pass_on(2 * b + AHEAD + 1, 1)
+            pass_on(2 * b + AHEAD + 2, 1)
+
         fill_band(b)
 
         @pl.when(b < 3)

time: 94 us -> 90.6 us (0.964)
  the two profiles are of different devices: /device:TPU:127 before, /device:TPU:105 now
where the time goes in v4:
time: 90.6 us; the launch traced here: 90.5 us
  Pallas kernels  87.7 us (97%)
  local copies, waits for them, and re-layouts  2.13 us (2%)
    pallas_call x1, Pallas kernels, per_device(): pl.pallas_call(functools.partial(kernel, (nd, nt, dates, bands, rows, col...  87.7 us
    unnamed x2, local copies, waits for them, and re-layouts  2.13 us

profile of v4, /device:TPU:105, one launch (start us, length us, event | category | flops | bytes accessed | tf_op | source)
XLA Modules:
  0.0 90.5 jit_solution(4683845402887150954)
XLA Ops:
  0.6 87.7 %fill_and_fit.1 = (bf16[9,10,8,1024]{3,2,1,0:T(8,128)(2,1)S(1)}, f32[12,24,8,128]{3,2,1,0:T(8,128)S(1)}) custom-call(bf16[9,10,8,1024]{3,2,1,0:T(8,128)(2,1)} %refl.1, s32[9,8,1024]{2,1,0:T(8,128)} %mask.1, f32[5]{0:T(128)} %time_k.1, f32[5]{0:T(128)} %space_k.1, bf16[384,576]{1,0:T(8,128)(2,1)} %constant.2.clone.fit_in), custom_call_target="tpu_custom_call" | custom-call | tf_op jit(solution)/shard_map/fill_and_fit/pallas_call | solution.py:466
  88.4 1.1 %copy.9 = bf16[9,10,8,1024]{3,2,1,0:T(8,128)(2,1)} copy(bf16[9,10,8,1024]{3,2,1,0:T(8,128)(2,1)S(1)} %get-tuple-element.2) | data formatting | bytes 2949120
  89.5 1.0 %copy.10 = f32[12,24,8,128]{3,2,1,0:T(8,128)} copy(f32[12,24,8,128]{3,2,1,0:T(8,128)S(1)} %get-tuple-element.3) | data formatting | bytes 2359296

commit v5 on v4

--- a/solution.py
+++ b/solution.py
@@ -445,6 +445,17 @@
         pltpu.make_async_copy(sent, sent, all_send.at[b]).wait()
 
 
+def hand_over(filled_in, coef_in, filled, coef, sem):
+    copies = [
+        pltpu.make_async_copy(filled_in, filled, sem.at[0]),
+        pltpu.make_async_copy(coef_in, coef, sem.at[1]),
+    ]
+    for copy in copies:
+        copy.start()
+    for copy in copies:
+        copy.wait()
+
+
 def solution(mesh):
     nd, nt = mesh.shape["date"], mesh.shape["tile"]
 
@@ -463,7 +474,7 @@
             jax.ShapeDtypeStruct((dates, bands, rows, cols), BF16),
             jax.ShapeDtypeStruct((bands + 2, TERMS, rows, width), F32),
         )
-        return pl.pallas_call(
+        results = pl.pallas_call(
             functools.partial(kernel, (nd, nt, dates, bands, rows, cols)),
             out_shape=tuple(pltpu.VMEM(s.shape, s.dtype) for s in shapes),
             in_specs=[anywhere, anywhere, scalars, scalars, anywhere],
@@ -502,6 +513,15 @@
             space_kernel,
             jnp.asarray(fit_operand(nd * dates, rows)),
         )
+        return pl.pallas_call(
+            hand_over,
+            out_shape=shapes,
+            in_specs=[anywhere, anywhere],
+            out_specs=(anywhere, anywhere),
+            scratch_shapes=[dma((2,))],
+            compiler_params=pltpu.CompilerParams(vmem_limit_bytes=2**20),
+            name="hand_over",
+        )(*results)
 
     placed = (P("date", None, "tile", None), P("date", "tile", None), P(), P())
     return jax.shard_map(

time: 90.6 us -> 90 us (level)
  local copies, waits for them, and re-layouts: 2.13 us -> 0 us
  Pallas kernels: 87.7 us -> 89.3 us
    unnamed x2 -> x0, local copies, waits for them, and re-layouts: 2.13 us -> none
    pallas_call x0 -> x1, Pallas kernels: none -> 1.52 us  [per_device(): pl.pallas_call(hand_over, out_shape=shapes, in_specs=[anywhere, anywhere]...]
where the time goes in v5:
time: 90 us; the launch traced here: 89.9 us
  Pallas kernels  89.3 us (99%)
    pallas_call x1, Pallas kernels, per_device(): pl.pallas_call(functools.partial(kernel, (nd, nt, dates, bands, rows, col...  87.7 us

profile of v5, /device:TPU:105, one launch (start us, length us, event | category | flops | bytes accessed | tf_op | source)
XLA Modules:
  0.0 89.9 jit_solution(7145711137845179476)
XLA Ops:
  0.6 87.7 %fill_and_fit.1 = (bf16[9,10,8,1024]{3,2,1,0:T(8,128)(2,1)S(1)}, f32[12,24,8,128]{3,2,1,0:T(8,128)S(1)}) custom-call(bf16[9,10,8,1024]{3,2,1,0:T(8,128)(2,1)} %refl.1, s32[9,8,1024]{2,1,0:T(8,128)} %mask.1, f32[5]{0:T(128)} %time_k.1, f32[5]{0:T(128)} %space_k.1, bf16[384,576]{1,0:T(8,128)(2,1)} %constant.2.clone.fit_in), custom_call_target="tpu_custom_call" | custom-call | tf_op jit(solution)/shard_map/fill_and_fit/pallas_call | solution.py:477
  88.4 1.5 %hand_over.1 = (bf16[9,10,8,1024]{3,2,1,0:T(8,128)(2,1)}, f32[12,24,8,128]{3,2,1,0:T(8,128)}) custom-call(bf16[9,10,8,1024]{3,2,1,0:T(8,128)(2,1)S(1)} %get-tuple-element.4.filled_in, f32[12,24,8,128]{3,2,1,0:T(8,128)S(1)} %get-tuple-element.5.coef_in), custom_call_target="tpu_custom_call" | custom-call | tf_op jit(solution)/shard_map/hand_over/pallas_call | solution.py:516
